TPU v7x, 32 devices: a whole 2x2x4 slice. The times are simulated.
32 devices in a mesh: dp: 8 (over z, core), tensor: 4 (over y, x).
Axes of the slice: x: 2, y: 2, z: 4, core: 2. Of those that a mesh axis runs over, the one named last changes fastest.
Arguments:
- inputs: bfloat16 [6144, 4096], P(('dp', 'tensor')), may hold values from -6 to 6
- cotangent: bfloat16 [6144, 4096], P(('dp', 'tensor')), may hold values from -6 to 6
- gate_pre: bfloat16 [6144, 14336], P('dp', 'tensor'), may hold values from -8 to 8
- up_pre: bfloat16 [6144, 14336], P('dp', 'tensor'), may hold values from -6 to 6
- w_down: bfloat16 [14336, 4096], P('tensor', 'dp'), may hold values from -0.046875 to 0.046875
- proj_model: bfloat16 [4096, 128], replicated, may hold values from -0.09375 to 0.09375
- proj_hidden: bfloat16 [14336, 128], P('tensor'), may hold values from -0.046875 to 0.046875
- queries: bfloat16 [256, 8192], P('tensor', 'dp'), may hold values from -0.125 to 0.125
- lengths: int32 [24], P('dp'), may hold values from 1 to 256, as said below
Outputs:
- scores: float32 [24, 256], P('dp', 'tensor')
Inputs may be any that keep to these rules, and one draw needn't show every extreme that they name: `lengths`: a route's real tokens fill its first slots, the rest are padding; some route has 256 and some route 1.
All inputs are finite; a program needn't handle non-finite values.
Results may differ from a plain program's by a relative error of at most 0.003.
Values may be sent and summed in bfloat16 or wider, within the bound.
A program may use at most 128 MiB of HBM per device.

v0:
```python
import math

import jax
import jax.numpy as jnp
from jax import lax
from jax.sharding import PartitionSpec as P


def route_weights(count, route_len, lengths, scale):
    position = jnp.arange(count, dtype=jnp.int32)
    owner = position // route_len
    within = position % route_len
    onehot = (owner[:, None] == jnp.arange(lengths.shape[0], dtype=jnp.int32)[None, :]).astype(
        jnp.float32
    )
    limit = jnp.sum(onehot * lengths.astype(jnp.float32)[None, :], axis=1)
    keep = (within.astype(jnp.float32) < limit).astype(jnp.float32) * scale
    return onehot * keep[:, None]


def route_features(weights, in_fac, up_fac, hid_fac, out_fac):
    count, routes = weights.shape
    rank = in_fac.shape[1]
    left_up = (weights[:, :, None] * in_fac[:, None, :]).reshape(count, routes * rank)
    grad_up = jnp.dot(left_up.T, up_fac, precision=lax.Precision.HIGHEST).reshape(
        routes, rank * rank
    )
    left_down = (weights[:, :, None] * hid_fac[:, None, :]).reshape(count, routes * rank)
    grad_down = jnp.dot(left_down.T, out_fac, precision=lax.Precision.HIGHEST).reshape(
        routes, rank * rank
    )
    return jnp.concatenate([grad_up, grad_down], axis=1)


def per_device(
    inputs, cotangent, gate_pre, up_pre, w_down, proj_model, proj_hidden, queries, lengths
):
    rank = proj_model.shape[1] // 2
    tok_dev = gate_pre.shape[0]
    route_len = tok_dev // lengths.shape[0]
    scale = 1.0 / math.sqrt(route_len)
    full_cot = lax.all_gather(cotangent, "tensor", axis=0, tiled=True)
    hidden_grad = lax.dot_general(
        full_cot,
        lax.all_gather(w_down, "dp", axis=1, tiled=True),
        (((1,), (1,)), ((), ())),
        preferred_element_type=jnp.float32,
    )
    gate_act = jax.nn.silu(gate_pre.astype(jnp.float32))
    hidden = (gate_act * up_pre.astype(jnp.float32)).astype(jnp.bfloat16)
    up_grad = (hidden_grad * gate_act).astype(jnp.bfloat16)
    up_part = jnp.dot(up_grad, proj_hidden[:, :rank], preferred_element_type=jnp.float32)
    hid_part = jnp.dot(hidden, proj_hidden[:, rank:], preferred_element_type=jnp.float32)
    query_rows = lax.all_gather(queries, "dp", axis=1, tiled=True)
    up_fac, hid_fac = lax.psum((up_part, hid_part), "tensor")
    in_local = jnp.dot(inputs, proj_model[:, :rank], preferred_element_type=jnp.float32)
    in_fac = lax.all_gather(in_local, "tensor", axis=0, tiled=True)
    out_fac = jnp.dot(full_cot, proj_model[:, rank:], preferred_element_type=jnp.float32)
    weights = route_weights(tok_dev, route_len, lengths, scale)
    features = route_features(weights, in_fac, up_fac, hid_fac, out_fac)
    return jnp.dot(features, query_rows.astype(jnp.float32).T, precision=lax.Precision.HIGHEST)


def solution(mesh):
    return jax.shard_map(
        per_device,
        mesh=mesh,
        in_specs=(
            P(("dp", "tensor"), None),
            P(("dp", "tensor"), None),
            P("dp", "tensor"),
            P("dp", "tensor"),
            P("tensor", "dp"),
            P(),
            P("tensor", None),
            P("tensor", "dp"),
            P("dp"),
        ),
        out_specs=P("dp", "tensor"),
        check_vma=False,
    )
```

profile of v0, /device:TPU:0, one launch (start us, length us, event | category | flops | bytes accessed | tf_op | source)
XLA Modules:
  0.0 448.4 jit_solution(17643671695243986657)
XLA Ops:
  6.5 0.0 copy-start
  6.5 0.0 all-gather.5.cloned.1.call-start
  6.5 0.7 all-gather.5.cloned.1.call-update
  7.3 0.0 all-gather.7.cloned.1.call-start
  7.3 0.7 all-gather.7.cloned.1.call-update
  8.0 0.0 all-reduce.3.cloned.1.call-start
  8.1 8.7 %fusion.3 = f32[768,64]{0,1:T(8,128)} fusion(bf16[768,3584]{1,0:T(8,128)(2,1)} %param.12, bf16[768,3584]{1,0:T(8,128)(2,1)} %param.11, bf16[3584,128]{1,0:T(8,128)(2,1)} %param.15), kind=kOutput, calls=%fused_computation.7 | convolution fusion | flops 374341632 | bytes 12124160 | tf_op jit(solution)/shard_map/dot_general | solution.py:53
  16.8 65.3 %all-gather.5.cloned.1.call-done = bf16[768,4096]{1,0:T(8,128)(2,1)} async-done(((bf16[192,4096]{1,0:T(8,128)(2,1)}), bf16[768,4096]{1,0:T(8,128)(2,1)}) %all-gather.5.cloned.1.call-update) | async-done | bytes 6291472 | tf_op jit(solution)/shard_map/all_gather | solution.py:42
  82.1 255.9 %all-gather.7.cloned.1.call-done = bf16[3584,4096]{1,0:T(8,128)(2,1)} async-done(((bf16[3584,512]{1,0:T(8,128)(2,1)}), bf16[3584,4096]{1,0:T(8,128)(2,1)}) %all-gather.7.cloned.1.call-update) | async-done | bytes 29360144 | tf_op jit(solution)/shard_map/all_gather | solution.py:45
  338.0 31.4 %multiply_convert_fusion.1 = bf16[768,3584]{1,0:T(8,128)(2,1)S(1)} fusion(bf16[768,4096]{1,0:T(8,128)(2,1)} %all-gather.5.cloned.1.call-done, bf16[3584,4096]{1,0:T(8,128)(2,1)} %all-gather.7.cloned.1.call-done, bf16[768,3584]{1,0:T(8,128)(2,1)} %param.11), kind=kOutput, calls=%fused_computation.6 | convolution fusion | flops 22567845888 | bytes 46661632 | tf_op jit(solution)/shard_map/dot_general | solution.py:43
  369.4 0.0 copy-done.2
  369.4 0.0 copy-start.1
  369.4 0.0 copy-start.3
  369.4 2.5 fusion.8
  371.9 0.0 all-reduce.3.cloned.1.call-update
  371.9 0.0 all-gather.9.cloned.1.call-start
  372.0 0.5 all-gather.9.cloned.1.call-update
  372.5 0.0 copy-done
  372.5 0.6 convolution_bitcast_fusion
  373.2 9.8 %all-gather = f32[4,192,64]{1,2,0:T(8,128)S(1)} all-gather(f32[1,192,64]{1,2,0:T(8,128)S(1)} %convolution_bitcast_fusion), channel_id=1, replica_groups=mesh['dp'=8,'tensor'=4] {'tensor'}, dimensions={0}, use_global_device_ids=true | all-gather | bytes 245760 | tf_op jit(solution)/shard_map/all_gather | solution.py:57
  383.0 0.2 copy.14
  383.1 0.2 reshape.82
  383.3 0.1 select_reduce_fusion
  383.4 4.9 %fusion.4 = f32[768,64]{0,1:T(8,128)S(1)} fusion(bf16[768,4096]{1,0:T(8,128)(2,1)} %all-gather.5.cloned.1.call-done, bf16[4096,128]{1,0:T(8,128)(2,1)S(1)} %copy-done.1), kind=kOutput, calls=%fused_computation.9 | convolution fusion | flops 402653184 | bytes 7536640 | tf_op jit(solution)/shard_map/dot_general | solution.py:58
  388.3 27.1 %all-reduce.3.cloned.1.call-done = (f32[768,64]{0,1:T(8,128)}, f32[768,64]{0,1:T(8,128)}) async-done(((f32[768,64]{0,1:T(8,128)}, f32[768,64]{0,1:T(8,128)}), (f32[768,64]{0,1:T(8,128)}, f32[768,64]{0,1:T(8,128)})) %all-reduce.3.cloned.1.call-update) | async-done | bytes 393232 | tf_op jit(solution)/shard_map/psum | solution.py:55
  415.4 1.0 broadcast_multiply_fusion.1
  416.4 1.5 fusion.27
  418.0 0.1 reshape.79
  418.1 0.6 fusion.28
  418.7 0.1 reshape.80
  418.8 20.3 %all-gather.9.cloned.1.call-done = bf16[64,8192]{1,0:T(8,128)(2,1)} async-done(((bf16[64,1024]{1,0:T(8,128)(2,1)}), bf16[64,8192]{1,0:T(8,128)(2,1)}) %all-gather.9.cloned.1.call-update) | async-done | bytes 1048592 | tf_op jit(solution)/shard_map/all_gather | solution.py:54
  439.1 2.7 fusion.10
  (7 shorter events, 0.0 us)
Async XLA Ops:
  6.5 366.0 %copy-start = (bf16[192,4096]{1,0:T(8,128)(2,1)S(1)}, bf16[192,4096]{1,0:T(8,128)(2,1)}, u32[]{:S(2)}) copy-start(bf16[192,4096]{1,0:T(8,128)(2,1)} %param.9) | copy-start | bytes 4718596
  6.5 75.6 %all-gather.5.cloned.1.call-start = ((), (), s32[]{:S(2)}) async-start(), calls=%async_computation | async-start | bytes 7864320 | tf_op jit(solution)/shard_map/all_gather | solution.py:42
  7.3 330.7 %all-gather.7.cloned.1.call-start = ((), (), s32[]{:S(2)}) async-start(), calls=%async_computation.1 | async-start | bytes 33030144 | tf_op jit(solution)/shard_map/all_gather | solution.py:45
  8.0 407.4 %all-reduce.3.cloned.1.call-start = ((), (), s32[]{:S(2)}) async-start(), calls=%async_computation.3 | async-start | bytes 786432 | tf_op jit(solution)/shard_map/psum | solution.py:55
  16.8 352.6 %copy-start.2 = (bf16[3584,128]{1,0:T(8,128)(2,1)S(1)}, bf16[3584,128]{1,0:T(8,128)(2,1)}, u32[]{:S(2)}) copy-start(bf16[3584,128]{1,0:T(8,128)(2,1)} %param.15) | copy-start | bytes 2752516
  369.4 3.1 copy-start.1
  369.4 3.8 copy-start.3
  371.9 67.2 %all-gather.9.cloned.1.call-start = ((), (), s32[]{:S(2)}) async-start(), calls=%async_computation.2 | async-start | bytes 1179648 | tf_op jit(solution)/shard_map/all_gather | solution.py:54
Sparse Core Ops, SparseCore 0:
  9.2 72.8 all-gather.4
  83.7 254.2 all-gather.6
  372.0 43.3 all-reduce.2
  417.0 22.0 all-gather.8
where the time goes:
time: 449 us; the launch traced here: 448 us
  waiting for transfers between devices  371 us (83%)
  matrix products  52.9 us (12%)
  between operations  13.3 us (3%)
  blocking collectives  9.79 us (2%)
    all_gather x1, waiting for transfers between devices, per_device(): lax.all_gather(w_down, 'dp', axis=1, tiled=True)  256 us
    all_gather x1, waiting for transfers between devices, per_device(): full_cot = lax.all_gather(cotangent, 'tensor', axis=0, tiled=True)  65.3 us
    dot_general x1, matrix products, per_device(): lax.dot_general(full_cot, lax.all_gather(w_down, 'dp', axis=1, tiled=True...  31.4 us
    psum x1, waiting for transfers between devices, per_device(): up_fac, hid_fac = lax.psum((up_part, hid_part), 'tensor')  27.1 us
    all_gather x1, waiting for transfers between devices, per_device(): query_rows = lax.all_gather(queries, 'dp', axis=1, tiled=True)  20.3 us
    all_gather x1, blocking collectives, per_device(): in_fac = lax.all_gather(in_local, 'tensor', axis=0, tiled=True)  9.79 us
  transfers between devices with their start and end apart: 4, of which 4 were waited for; matrix products, arithmetic and copies ran while one was open for 4% of the time, Pallas kernels for 0%

commit v1 on v0

v1 whole, which is shorter than its diff:
```python
import functools
import math

import jax
import jax.numpy as jnp
from jax import lax
from jax.experimental import pallas as pl
from jax.experimental.pallas import tpu as pltpu
from jax.sharding import PartitionSpec as P

MESH = pl.DeviceIdType.MESH
WINDOW = 4
AHEAD = 2


def both(*terms):
    out = terms[0]
    for term in terms[1:]:
        out = jnp.logical_and(out, term)
    return out


def silu(v):
    return v / (1.0 + jnp.exp(-v))


def kernel(
    N, T, K, F, START,
    x_ref, cot_ref, gate_ref, up_ref, w_ref, pm_ref, ph_ref, q_ref,
    up_out, hid_out, in_out, outf_out, q_all,
    w_all, cot_all, ext_cot, gate_v, up_v, ext_gate, ext_acc, ret, x_v, pm_v, ph_v,
    bulk, up_sem, w_snd, w_rcv, q_snd, q_rcv, c_snd, c_rcv, f_snd, f_rcv, e_snd, e_rcv, g_snd, g_rcv, r_sem,
):
    dp = lax.axis_index("dp")
    t = lax.axis_index("tensor")
    z = dp // 2
    c = dp % 2
    R, cols = w_all.shape[1], w_ref.shape[2]
    mb = cot_ref.shape[0]
    qc = q_ref.shape[1]
    E = K - F
    above, below, sib = (dp + 2, t), (dp - 2, t), (dp + 1 - 2 * c, t)
    peers = [(dp, (t + d) % T) for d in range(1, T)]
    low_end, high_end = z == 0, z == N - 1
    at_end = jnp.logical_or(low_end, high_end)
    host = jnp.logical_or(z == 1, z == N - 2)

    rows = pl.ds(pl.multiple_of(t * mb, mb), mb)

    def w_cols(plane, core):
        return pl.ds(pl.multiple_of((2 * plane + core) * cols, cols), cols)

    def q_cols(plane, core):
        return pl.ds(pl.multiple_of((2 * plane + core) * qc, qc), qc)

    loads = [
        pltpu.make_async_copy(x_ref, x_v, bulk.at[0]),
        pltpu.make_async_copy(pm_ref, pm_v, bulk.at[1]),
        pltpu.make_async_copy(gate_ref, gate_v, bulk.at[2]),
        pltpu.make_async_copy(ph_ref, ph_v, bulk.at[3]),
        pltpu.make_async_copy(cot_ref, cot_all.at[rows], bulk.at[4]),
        pltpu.make_async_copy(q_ref, q_all.at[:, q_cols(z, c)], bulk.at[5]),
        pltpu.make_async_copy(w_ref, w_all.at[:, :, w_cols(z, c)], bulk.at[6]),
    ]
    for load in loads:
        load.start()

    barrier = pltpu.get_barrier_semaphore()
    for peer in [sib] + peers:
        pl.semaphore_signal(barrier, inc=1, device_id=peer, device_id_type=MESH)
    for cond, peer in ((z < N - 1, above), (z > 0, below)):

        @pl.when(cond)
        def _():
            pl.semaphore_signal(barrier, inc=1, device_id=peer, device_id_type=MESH)

    pl.semaphore_wait(barrier, T + 2 - (z + 1) // N - (N - z) // N)

    def remote(src, dst, ssem, rsem, peer):
        return pltpu.make_async_remote_copy(
            src_ref=src, dst_ref=dst, send_sem=ssem, recv_sem=rsem, device_id=peer, device_id_type=MESH
        )

    ends = ((low_end, above), (high_end, below))
    e_out = [remote(cot_ref, ext_cot.at[rows], e_snd.at[0], e_rcv.at[0], peer) for _, peer in ends]
    if E:
        for (cond, _), copy in zip(ends, e_out):
            pl.when(cond)(copy.start)

    def mine(k):
        return jnp.logical_or(jnp.logical_not(at_end), k < F)

    def go_up(k):
        return jnp.logical_and(z < N - 1, jnp.logical_or(z + 1 < N - 1, k < F))

    def go_down(k):
        return jnp.logical_and(z > 0, jnp.logical_or(z - 1 > 0, k < F))

    def w_push(index, src_of, plane, cond_of, peer, k, start=True):
        def copy(j):
            return remote(
                src_of(j),
                w_all.at[j, :, w_cols(plane, c)],
                w_snd.at[index, j % WINDOW],
                w_rcv.at[2 * plane + c, j],
                peer,
            )

        @pl.when(both(k >= WINDOW, k < K + WINDOW, cond_of(k - WINDOW)))
        def _():
            copy(k - WINDOW).wait_send()

        if start:

            @pl.when(both(k < K, cond_of(k)))
            def _():
                copy(k).start()

    def own(k, start=True):
        src = lambda j: w_ref.at[j]
        w_push(0, src, z, go_up, above, k, start)
        w_push(N, src, z, go_down, below, k, start)
        w_push(2 * N, src, z, mine, sib, k, start)

    def relay(k, start=True):
        for d in range(1, N):
            for upward in (True, False):
                plane = z - d if upward else z + d
                valid = plane >= 0 if upward else plane <= N - 1
                got = lambda j, valid=valid: jnp.logical_and(valid, mine(j))
                go = go_up if upward else go_down
                onward = lambda j, valid=valid, go=go: jnp.logical_and(valid, go(j))
                src = lambda j, plane=plane: w_all.at[j, :, w_cols(plane, c)]
                if start:

                    @pl.when(got(k))
                    def _():
                        remote(
                            src(k), src(k), w_snd.at[0, 0], w_rcv.at[2 * plane + c, k], sib
                        ).wait_recv()

                base = 0 if upward else N
                w_push(base + d, src, plane, onward, above if upward else below, k, start)
                w_push(2 * N + base + d, src, plane, got, sib, k, start)

    def q_copy(index, src, plane, peer):
        return remote(
            src, q_all.at[:, q_cols(plane, c)], q_snd.at[index], q_rcv.at[2 * plane + c], peer
        )

    def q_own(method):
        for index, cond, peer in ((0, z < N - 1, above), (N, z > 0, below), (2 * N, None, sib)):
            copy = q_copy(index, q_ref, z, peer)
            act = copy.start if method == "start" else copy.wait_send
            act() if cond is None else pl.when(cond)(act)

    def q_relay(method):
        for d in range(1, N):
            for upward in (True, False):
                plane = z - d if upward else z + d
                valid = plane >= 0 if upward else plane <= N - 1
                base = 0 if upward else N
                src = q_all.at[:, q_cols(plane, c)]
                far = z < N - 1 if upward else z > 0
                onward = q_copy(base + d, src, plane, above if upward else below)
                over = q_copy(2 * N + base + d, src, plane, sib)

                @pl.when(valid)
                def _():
                    if method == "start":
                        over.wait_recv()
                        over.start()
                        pl.when(far)(onward.start)
                    else:
                        over.wait_send()
                        pl.when(far)(onward.wait_send)

    for k in range(min(AHEAD, K)):
        own(jnp.int32(k))

    c_out = [
        remote(cot_ref, cot_all.at[rows], c_snd.at[d], c_rcv.at[d], peer) for d, peer in enumerate(peers)
    ]
    for copy in c_out:
        copy.start()
    q_own("start")

    loads[0].wait()
    loads[1].wait()
    in_out[rows, :] = jnp.dot(x_v[...], pm_v[...], preferred_element_type=jnp.float32)
    f_out = [
        remote(in_out.at[rows], in_out.at[rows], f_snd.at[d], f_rcv.at[d], peer)
        for d, peer in enumerate(peers)
    ]
    for copy in f_out:
        copy.start()
    for load in loads[2:]:
        load.wait()

    up_out[...] = jnp.zeros_like(up_out)
    hid_out[...] = jnp.zeros_like(hid_out)
    ext_acc[...] = jnp.zeros_like(ext_acc)

    def lanes(k):
        return pl.ds(pl.multiple_of(k * R, R), R)

    def up_load(k):
        return pltpu.make_async_copy(up_ref.at[:, lanes(k)], up_v.at[k % 2], up_sem.at[k % 2])

    up_load(jnp.int32(0)).start()

    def hid(k):
        @pl.when(k + 1 < K)
        def _():
            up_load(k + 1).start()

        up_load(k).wait()
        act = silu(gate_v[:, lanes(k)].astype(jnp.float32))
        hidden = (act * up_v[k % 2].astype(jnp.float32)).astype(jnp.bfloat16)
        hid_out[...] += jnp.dot(hidden, ph_v[k], preferred_element_type=jnp.float32)

    def product(cot, act, k, total):
        grad = lax.dot_general(
            cot[...], w_all[k], (((1,), (1,)), ((), ())), preferred_element_type=jnp.float32
        )
        up_grad = (grad * act).astype(jnp.bfloat16)
        total[...] += jnp.dot(up_grad, ph_v[k], preferred_element_type=jnp.float32)

    def main(k):
        @pl.when(mine(k))
        def _():
            for plane in range(N):
                ref = w_all.at[k, :, w_cols(plane, 1 - c)]
                remote(ref, ref, w_snd.at[0, 0], w_rcv.at[2 * plane + 1 - c, k], sib).wait_recv()
            product(cot_all, silu(gate_v[:, lanes(k)].astype(jnp.float32)), k, up_out)

    def ext(j):
        ref = ext_gate.at[j]
        remote(ref, ref, g_snd.at[j], g_rcv.at[j], sib).wait_recv()
        product(ext_cot, silu(ref[...].astype(jnp.float32)), F + j, ext_acc)

    e_on = [
        remote(ext_cot.at[rows], ext_cot.at[rows], e_snd.at[d], e_rcv.at[d], peer)
        for d, peer in enumerate(peers, 1)
    ]

    def g_copy(j, peer):
        return remote(gate_ref.at[:, lanes(F + j)], ext_gate.at[j], g_snd.at[j], g_rcv.at[j], peer)

    def step(s, carry):
        own(s + AHEAD)
        if E:
            for cond, peer in ends:

                @pl.when(both(cond, s % 2 == 0, s // 2 < E))
                def _():
                    g_copy(s // 2, peer).start()

            @pl.when(both(host, s == 2))
            def _():
                e_out[0].wait_recv()
                for copy in e_on:
                    copy.start()

        relay(s)

        @pl.when(s == 1)
        def _():
            q_relay("start")

        hid(s)

        @pl.when(s == START)
        def _():
            for copy in c_out:
                copy.wait_recv()
            outf_out[...] = jnp.dot(cot_all[...], pm_v[...], preferred_element_type=jnp.float32)

        def catch_up(i, carry):
            k = 2 * (s - START) + i

            @pl.when(both(k >= 0, k < s))
            def _():
                main(k)

            return carry

        lax.fori_loop(0, 2, catch_up, 0)
        return carry

    lax.fori_loop(0, K, step, 0)

    def rest(k, carry):
        main(k)
        return carry

    lax.fori_loop(min(2 * (K - START), K - 1), K, rest, 0)

    if E:

        @pl.when(host)
        def _():
            for copy in e_on:
                copy.wait_recv()
            lax.fori_loop(0, E, lambda j, carry: (ext(j), carry)[1], 0)

        r_out = [remote(ext_acc, ret, r_sem.at[0], r_sem.at[1], peer) for peer in (below, above)]
        for cond, copy in zip((z == 1, z == N - 2), r_out):
            pl.when(cond)(copy.start)

        @pl.when(at_end)
        def _():
            r_out[0].wait_recv()
            up_out[...] += ret[...]

        for cond, copy in zip((z == 1, z == N - 2), r_out):
            pl.when(cond)(copy.wait_send)

        @pl.when(host)
        def _():
            for copy in e_on:
                copy.wait_send()

        for (cond, peer), copy in zip(ends, e_out):

            @pl.when(cond)
            def _():
                copy.wait_send()
                for j in range(E):
                    g_copy(j, peer).wait_send()

    for copy in f_out + c_out:
        copy.wait_send()
    for copy in f_out:
        copy.wait_recv()
    for plane in range(N):
        ref = q_all.at[:, q_cols(plane, 1 - c)]
        remote(ref, ref, q_snd.at[0], q_rcv.at[2 * plane + 1 - c], sib).wait_recv()
    q_own("wait")
    q_relay("wait")

    def drain_own(k, carry):
        own(k, False)
        return carry

    def drain_relay(k, carry):
        relay(k, False)
        return carry

    lax.fori_loop(K + AHEAD, K + WINDOW, drain_own, 0)
    lax.fori_loop(K, K + WINDOW, drain_relay, 0)


def gather_and_project(N, T, x, cot, gate, up, w, pm, ph, q):
    tokens, hidden = gate.shape
    R = 256 if hidden % 256 == 0 else 128
    K = hidden // R
    F = K if N < 4 else -(-9 * K // 14)
    E = max(K - F, 1)
    D = cot.shape[1]
    width = pm.shape[1]
    start = K // 2
    f32, bf16 = jnp.float32, jnp.bfloat16
    dma = pltpu.SemaphoreType.DMA
    vmem = pl.BlockSpec(memory_space=pltpu.VMEM)
    return pl.pallas_call(
        functools.partial(kernel, N, T, K, F, start),
        out_shape=[jax.ShapeDtypeStruct((tokens, width), f32)] * 4
        + [jax.ShapeDtypeStruct((q.shape[0], 2 * N * q.shape[1]), bf16)],
        in_specs=[pl.BlockSpec(memory_space=pl.ANY)] * 8,
        out_specs=[vmem] * 5,
        scratch_shapes=[
            pltpu.VMEM((K, R, D), bf16),
            pltpu.VMEM((tokens, D), bf16),
            pltpu.VMEM((tokens, D), bf16),
            pltpu.VMEM((tokens, hidden), bf16),
            pltpu.VMEM((2, tokens, R), bf16),
            pltpu.VMEM((E, tokens, R), bf16),
            pltpu.VMEM((tokens, width), f32),
            pltpu.VMEM((tokens, width), f32),
            pltpu.VMEM(x.shape, bf16),
            pltpu.VMEM(pm.shape, bf16),
            pltpu.VMEM((K, R, width), bf16),
            dma((7,)),
            dma((2,)),
            dma((4 * N, WINDOW)),
            dma((2 * N, K)),
            dma((4 * N,)),
            dma((2 * N,)),
            dma((T,)),
            dma((T,)),
            dma((T,)),
            dma((T,)),
            dma((T,)),
            dma((T,)),
            dma((E,)),
            dma((E,)),
            dma((2,)),
        ],
        compiler_params=pltpu.CompilerParams(
            collective_id=0, has_side_effects=True, vmem_limit_bytes=61 * 1024 * 1024
        ),
    )(x, cot, gate, up, w.reshape(K, R, w.shape[1]), pm, ph.reshape(K, R, width), q)


def route_features(keep, left, right):
    routes, count = keep.shape
    rank = left.shape[1]
    left = (left.reshape(routes, count, rank) * keep[:, :, None])
    right = right.reshape(routes, count, rank)
    return jnp.einsum("eti,etj->eij", left, right, precision=lax.Precision.HIGHEST).reshape(
        routes, rank * rank
    )


def per_device(
    N, T, inputs, cotangent, gate_pre, up_pre, w_down, proj_model, proj_hidden, queries, lengths
):
    rank = proj_model.shape[1] // 2
    routes = lengths.shape[0]
    route_len = gate_pre.shape[0] // routes
    up_part, hid_part, in_fac, out_fac, query_rows = gather_and_project(
        N, T, inputs, cotangent, gate_pre, up_pre, w_down, proj_model, proj_hidden, queries
    )
    scale = 1.0 / math.sqrt(route_len)
    position = jnp.arange(route_len, dtype=jnp.int32)
    keep = (position[None, :] < lengths[:, None]).astype(jnp.float32) * scale
    part = jnp.concatenate(
        [
            route_features(keep, in_fac[:, :rank], up_part[:, :rank]),
            route_features(keep, hid_part[:, rank:], out_fac[:, rank:]),
        ],
        axis=1,
    )
    features = lax.psum(part, "tensor")
    return jnp.dot(features, query_rows.astype(jnp.float32).T, precision=lax.Precision.HIGHEST)


def solution(mesh):
    return jax.shard_map(
        functools.partial(per_device, mesh.shape["dp"] // 2, mesh.shape["tensor"]),
        mesh=mesh,
        in_specs=(
            P(("dp", "tensor"), None),
            P(("dp", "tensor"), None),
            P("dp", "tensor"),
            P("dp", "tensor"),
            P("tensor", "dp"),
            P(),
            P("tensor", None),
            P("tensor", "dp"),
            P("dp"),
        ),
        out_specs=P("dp", "tensor"),
        check_vma=False,
    )
```

time: 449 us -> 330 us (0.73)
  waiting for transfers between devices: 371 us -> 41.8 us
  Pallas kernels: 0 us -> 266 us
  matrix products: 52.9 us -> 4.15 us
  blocking collectives: 9.79 us -> 0 us
    all_gather x3 -> x0, waiting for transfers between devices: 341 us -> none  [the longest x1 256 us: per_device(): lax.all_gather(w_down, 'dp', axis=1, tiled=True)]
    pallas_call x0 -> x1, Pallas kernels: none -> 266 us  [gather_and_project(): pl.pallas_call(functools.partial(kernel, N, T, K, F, start), out_shape=[j...]
    dot_general x7 -> x2, matrix products: 50.2 us -> 1.74 us  [route_features(): jnp.einsum('eti,etj->eij', left, right, precision=lax.Precision.HIGHEST)]
    psum x1, waiting for transfers between devices: 27.1 us -> 41.8 us  [per_device(): features = lax.psum(part, 'tensor')]
    all_gather x1 -> x0, blocking collectives: 9.79 us -> none  [per_device(): in_fac = lax.all_gather(in_local, 'tensor', axis=0, tiled=True)]
  transfers between devices with their start and end apart: 4 -> 1, of which waited for: 4 -> 1; matrix products, arithmetic and copies ran while one was open for 4% -> 0% of each run, Pallas kernels for 0% -> 0%
where the time goes in v1:
time: 330 us
  Pallas kernels  266 us (81%)
  waiting for transfers between devices  41.8 us (13%)
  between operations  13.5 us (4%)
  matrix products  4.15 us (1%)
  local copies, waits for them, and re-layouts  3.9 us (1%)
    pallas_call x1, Pallas kernels, gather_and_project(): pl.pallas_call(functools.partial(kernel, N, T, K, F, start), out_shape=[j...  266 us
    psum x1, waiting for transfers between devices, per_device(): features = lax.psum(part, 'tensor')  41.8 us
  transfers between devices with their start and end apart: 1, of which 1 were waited for; matrix products, arithmetic and copies ran while one was open for 0% of the time, Pallas kernels for 0%

profile of v1, /device:TPU:0, one launch (start us, length us, event | category | flops | bytes accessed | tf_op | source)
XLA Modules:
  0.0 329.6 jit_solution(16964315201585670038)
XLA Ops:
  6.5 0.0 all-reduce.2.cloned.1.call-start
  6.5 0.0 copy-start.1
  6.5 265.6 %shard_map.91 = (f32[768,128]{1,0:T(8,128)}, f32[768,128]{1,0:T(8,128)}, f32[768,128]{1,0:T(8,128)}, f32[768,128]{1,0:T(8,128)}, bf16[64,8192]{1,0:T(8,128)(2,1)}) custom-call(bf16[192,4096]{1,0:T(8,128)(2,1)} %x_ref.1, bf16[192,4096]{1,0:T(8,128)(2,1)} %cot_ref.1, bf16[768,3584]{1,0:T(8,128)(2,1)} %gate_ref.1, bf16[768,3584]{1,0:T(8,128)(2,1)} %up_ref.1, ...), custom_call_target="tpu_custom_call" | custom-call | tf_op jit(solution)/shard_map/pallas_call | solution.py:366
  272.1 0.0 copy-start
  272.2 1.2 copy.10
  273.4 0.0 copy-done.1
  273.4 0.1 fusion.6
  273.5 1.4 fusion.2
  274.8 0.1 reshape.50
  274.9 1.2 slice.14
  276.1 0.1 copy.12
  276.3 1.2 slice.15
  277.4 0.4 fusion
  277.8 0.1 reshape.53
  277.9 0.7 pad_maximum_fusion
  278.6 0.0 all-reduce.2.cloned.1.call-update
  278.6 41.8 %all-reduce.2.cloned.1.call-done = f32[3,8192]{1,0:T(4,128)} async-done(((f32[3,8192]{1,0:T(4,128)}), f32[3,8192]{1,0:T(4,128)}) %all-reduce.2.cloned.1.call-update) | async-done | bytes 98320 | tf_op jit(solution)/shard_map/psum | solution.py:435
  320.4 0.0 copy-done
  320.4 2.4 fusion.7
Async XLA Ops:
  6.5 313.9 %all-reduce.2.cloned.1.call-start = ((), (), s32[]{:S(2)}) async-start(), calls=%async_computation | async-start | bytes 262144 | tf_op jit(solution)/shard_map/psum | solution.py:435
  6.5 266.9 %copy-start.1 = (s32[3]{0:T(128)S(1)}, s32[3]{0:T(128)}, u32[]{:S(2)}) copy-start(s32[3]{0:T(128)} %param.17) | copy-start | bytes 40
  272.1 48.3 %copy-start = (bf16[64,8192]{1,0:T(8,128)(2,1)S(1)}, bf16[64,8192]{1,0:T(8,128)(2,1)}, u32[]{:S(2)}) copy-start(bf16[64,8192]{1,0:T(8,128)(2,1)} %get-tuple-element.14) | copy-start | bytes 3145732
Sparse Core Ops, SparseCore 0:
  278.7 41.6 all-reduce.1

commit v2 on v1

--- a/solution.py
+++ b/solution.py
@@ -9,8 +9,9 @@
 from jax.sharding import PartitionSpec as P
 
 MESH = pl.DeviceIdType.MESH
-WINDOW = 4
-AHEAD = 2
+WINDOW = 14
+AHEAD = 4
+EARLY = 5
 
 
 def both(*terms):
@@ -26,10 +27,10 @@
 
 def kernel(
     N, T, K, F, START,
-    x_ref, cot_ref, gate_ref, up_ref, w_ref, pm_ref, ph_ref, q_ref,
-    up_out, hid_out, in_out, outf_out, q_all,
-    w_all, cot_all, ext_cot, gate_v, up_v, ext_gate, ext_acc, ret, x_v, pm_v, ph_v,
-    bulk, up_sem, w_snd, w_rcv, q_snd, q_rcv, c_snd, c_rcv, f_snd, f_rcv, e_snd, e_rcv, g_snd, g_rcv, r_sem,
+    x_ref, cot_ref, gate_ref, up_ref, w_ref, pm_ref, ph_ref, q_ref, len_ref,
+    feat_out, q_all,
+    up_out, hid_out, in_out, outf_out, part, parts, w_all, cot_all, ext_cot, gate_v, up_v, ext_gate, ext_acc, ret, x_v, pm_v, ph_v,
+    bulk, up_sem, w_snd, w_rcv, q_snd, q_rcv, c_snd, c_rcv, f_snd, f_rcv, e_snd, e_rcv, g_snd, g_rcv, r_sem, p_snd, p_rcv,
 ):
     dp = lax.axis_index("dp")
     t = lax.axis_index("tensor")
@@ -44,6 +45,7 @@
     low_end, high_end = z == 0, z == N - 1
     at_end = jnp.logical_or(low_end, high_end)
     host = jnp.logical_or(z == 1, z == N - 2)
+    EVEN = 2 * START - N + 1
 
     rows = pl.ds(pl.multiple_of(t * mb, mb), mb)
 
@@ -106,13 +108,15 @@
                 peer,
             )
 
-        @pl.when(both(k >= WINDOW, k < K + WINDOW, cond_of(k - WINDOW)))
+        most = K if start else K + WINDOW
+
+        @pl.when(both(k >= WINDOW, k < most, cond_of(k - WINDOW)))
         def _():
             copy(k - WINDOW).wait_send()
 
         if start:
 
-            @pl.when(both(k < K, cond_of(k)))
+            @pl.when(both(k >= 0, k < K, cond_of(k)))
             def _():
                 copy(k).start()
 
@@ -122,8 +126,9 @@
         w_push(N, src, z, go_down, below, k, start)
         w_push(2 * N, src, z, mine, sib, k, start)
 
-    def relay(k, start=True):
+    def relay(first, start=True):
         for d in range(1, N):
+            k = first - d + 1 if start else first
             for upward in (True, False):
                 plane = z - d if upward else z + d
                 valid = plane >= 0 if upward else plane <= N - 1
@@ -133,7 +138,7 @@
                 src = lambda j, plane=plane: w_all.at[j, :, w_cols(plane, c)]
                 if start:
 
-                    @pl.when(got(k))
+                    @pl.when(both(k >= 0, k < K, got(k)))
                     def _():
                         remote(
                             src(k), src(k), w_snd.at[0, 0], w_rcv.at[2 * plane + c, k], sib
@@ -154,8 +159,8 @@
             act = copy.start if method == "start" else copy.wait_send
             act() if cond is None else pl.when(cond)(act)
 
-    def q_relay(method):
-        for d in range(1, N):
+    def q_relay(method, distances):
+        for d in distances:
             for upward in (True, False):
                 plane = z - d if upward else z + d
                 valid = plane >= 0 if upward else plane <= N - 1
@@ -256,7 +261,7 @@
                 def _():
                     g_copy(s // 2, peer).start()
 
-            @pl.when(both(host, s == 2))
+            @pl.when(both(host, s == EARLY))
             def _():
                 e_out[0].wait_recv()
                 for copy in e_on:
@@ -264,11 +269,13 @@
 
         relay(s)
 
-        @pl.when(s == 1)
-        def _():
-            q_relay("start")
-
-        hid(s)
+        for d in range(1, N):
+
+            @pl.when(s == d + 2)
+            def _():
+                q_relay("start", [d])
+
+        pl.when(s < K)(functools.partial(hid, s))
 
         @pl.when(s == START)
         def _():
@@ -278,23 +285,17 @@
 
         def catch_up(i, carry):
             k = 2 * (s - START) + i
-
-            @pl.when(both(k >= 0, k < s))
-            def _():
-                main(k)
-
+            pl.when(k < K)(functools.partial(main, k))
             return carry
 
-        lax.fori_loop(0, 2, catch_up, 0)
+        @pl.when(both(s >= START, s < EVEN))
+        def _():
+            lax.fori_loop(0, 2, catch_up, 0)
+
+        pl.when(both(s >= EVEN, s - N + 1 < K))(lambda: main(s - N + 1))
         return carry
 
-    lax.fori_loop(0, K, step, 0)
-
-    def rest(k, carry):
-        main(k)
-        return carry
-
-    lax.fori_loop(min(2 * (K - START), K - 1), K, rest, 0)
+    lax.fori_loop(0, K + N - 2, step, 0)
 
     if E:
 
@@ -302,8 +303,12 @@
         def _():
             for copy in e_on:
                 copy.wait_recv()
-            lax.fori_loop(0, E, lambda j, carry: (ext(j), carry)[1], 0)
-
+            lax.fori_loop(0, E - 1, lambda j, carry: (ext(j), carry)[1], 0)
+
+    main(K - 1)
+
+    if E:
+        pl.when(host)(lambda: ext(E - 1))
         r_out = [remote(ext_acc, ret, r_sem.at[0], r_sem.at[1], peer) for peer in (below, above)]
         for cond, copy in zip((z == 1, z == N - 2), r_out):
             pl.when(cond)(copy.start)
@@ -312,6 +317,37 @@
         def _():
             r_out[0].wait_recv()
             up_out[...] += ret[...]
+
+    for copy in f_out:
+        copy.wait_recv()
+    routes = len_ref.shape[0]
+    span = up_out.shape[0] // routes
+    rank = up_out.shape[1] // 2
+    position = lax.broadcasted_iota(jnp.int32, (span, 2 * rank), 0)
+    lane = lax.broadcasted_iota(jnp.int32, (rank, 2 * rank), 1)
+
+    def outer(left, right):
+        return lax.dot_general(
+            left,
+            right,
+            (((0,), (0,)), ((), ())),
+            precision=lax.Precision.HIGHEST,
+            preferred_element_type=jnp.float32,
+        )
+
+    for e in range(routes):
+        at = pl.ds(e * span, span)
+        keep = jnp.where(position < len_ref[e], 1.0 / math.sqrt(span), 0.0).astype(jnp.float32)
+        grad_up = outer(in_out[at, :] * keep, up_out[at, :])
+        grad_down = outer(hid_out[at, :] * keep, outf_out[at, :])
+        part[pl.ds(e * rank, rank), :] = jnp.where(lane < rank, grad_up[:rank], grad_down[rank:])
+    p_out = [
+        remote(part, parts.at[d], p_snd.at[d], p_rcv.at[d], peer) for d, peer in enumerate(peers)
+    ]
+    for copy in p_out:
+        copy.start()
+
+    if E:
 
         for cond, copy in zip((z == 1, z == N - 2), r_out):
             pl.when(cond)(copy.wait_send)
@@ -331,13 +367,11 @@
 
     for copy in f_out + c_out:
         copy.wait_send()
-    for copy in f_out:
-        copy.wait_recv()
     for plane in range(N):
         ref = q_all.at[:, q_cols(plane, 1 - c)]
         remote(ref, ref, q_snd.at[0], q_rcv.at[2 * plane + 1 - c], sib).wait_recv()
     q_own("wait")
-    q_relay("wait")
+    q_relay("wait", range(1, N))
 
     def drain_own(k, carry):
         own(k, False)
@@ -347,11 +381,19 @@
         relay(k, False)
         return carry
 
-    lax.fori_loop(K + AHEAD, K + WINDOW, drain_own, 0)
+    lax.fori_loop(K, K + WINDOW, drain_own, 0)
     lax.fori_loop(K, K + WINDOW, drain_relay, 0)
 
-
-def gather_and_project(N, T, x, cot, gate, up, w, pm, ph, q):
+    total = part[...]
+    for d, copy in enumerate(p_out):
+        copy.wait_recv()
+        total = total + parts[d]
+    feat_out[...] = total
+    for copy in p_out:
+        copy.wait_send()
+
+
+def gather_and_project(N, T, x, cot, gate, up, w, pm, ph, q, lengths):
     tokens, hidden = gate.shape
     R = 256 if hidden % 256 == 0 else 128
     K = hidden // R
@@ -359,17 +401,26 @@
     E = max(K - F, 1)
     D = cot.shape[1]
     width = pm.shape[1]
-    start = K // 2
+    start = max(K // 2 + 1, N)
     f32, bf16 = jnp.float32, jnp.bfloat16
     dma = pltpu.SemaphoreType.DMA
     vmem = pl.BlockSpec(memory_space=pltpu.VMEM)
     return pl.pallas_call(
         functools.partial(kernel, N, T, K, F, start),
-        out_shape=[jax.ShapeDtypeStruct((tokens, width), f32)] * 4
-        + [jax.ShapeDtypeStruct((q.shape[0], 2 * N * q.shape[1]), bf16)],
-        in_specs=[pl.BlockSpec(memory_space=pl.ANY)] * 8,
-        out_specs=[vmem] * 5,
+        out_shape=[
+            jax.ShapeDtypeStruct((lengths.shape[0] * width // 2, width), f32),
+            jax.ShapeDtypeStruct((q.shape[0], 2 * N * q.shape[1]), bf16),
+        ],
+        in_specs=[pl.BlockSpec(memory_space=pl.ANY)] * 8
+        + [pl.BlockSpec(memory_space=pltpu.SMEM)],
+        out_specs=[vmem] * 2,
         scratch_shapes=[
+            pltpu.VMEM((tokens, width), f32),
+            pltpu.VMEM((tokens, width), f32),
+            pltpu.VMEM((tokens, width), f32),
+            pltpu.VMEM((tokens, width), f32),
+            pltpu.VMEM((lengths.shape[0] * width // 2, width), f32),
+            pltpu.VMEM((T, lengths.shape[0] * width // 2, width), f32),
             pltpu.VMEM((K, R, D), bf16),
             pltpu.VMEM((tokens, D), bf16),
             pltpu.VMEM((tokens, D), bf16),
@@ -396,21 +447,13 @@
             dma((E,)),
             dma((E,)),
             dma((2,)),
+            dma((T,)),
+            dma((T,)),
         ],
         compiler_params=pltpu.CompilerParams(
             collective_id=0, has_side_effects=True, vmem_limit_bytes=61 * 1024 * 1024
         ),
-    )(x, cot, gate, up, w.reshape(K, R, w.shape[1]), pm, ph.reshape(K, R, width), q)
-
-
-def route_features(keep, left, right):
-    routes, count = keep.shape
-    rank = left.shape[1]
-    left = (left.reshape(routes, count, rank) * keep[:, :, None])
-    right = right.reshape(routes, count, rank)
-    return jnp.einsum("eti,etj->eij", left, right, precision=lax.Precision.HIGHEST).reshape(
-        routes, rank * rank
-    )
+    )(x, cot, gate, up, w.reshape(K, R, w.shape[1]), pm, ph.reshape(K, R, width), q, lengths)
 
 
 def per_device(
@@ -418,21 +461,10 @@
 ):
     rank = proj_model.shape[1] // 2
     routes = lengths.shape[0]
-    route_len = gate_pre.shape[0] // routes
-    up_part, hid_part, in_fac, out_fac, query_rows = gather_and_project(
-        N, T, inputs, cotangent, gate_pre, up_pre, w_down, proj_model, proj_hidden, queries
+    features, query_rows = gather_and_project(
+        N, T, inputs, cotangent, gate_pre, up_pre, w_down, proj_model, proj_hidden, queries, lengths
     )
-    scale = 1.0 / math.sqrt(route_len)
-    position = jnp.arange(route_len, dtype=jnp.int32)
-    keep = (position[None, :] < lengths[:, None]).astype(jnp.float32) * scale
-    part = jnp.concatenate(
-        [
-            route_features(keep, in_fac[:, :rank], up_part[:, :rank]),
-            route_features(keep, hid_part[:, rank:], out_fac[:, rank:]),
-        ],
-        axis=1,
-    )
-    features = lax.psum(part, "tensor")
+    features = features.reshape(routes, rank, 2, rank).transpose(0, 2, 1, 3).reshape(routes, -1)
     return jnp.dot(features, query_rows.astype(jnp.float32).T, precision=lax.Precision.HIGHEST)
 
 

time: 330 us -> 221 us (0.67)
  Pallas kernels: 266 us -> 216 us
  waiting for transfers between devices: 41.8 us -> 0 us
  between operations: 13.5 us -> 0.03 us
    pallas_call x1, Pallas kernels: 266 us -> 216 us  [gather_and_project(): pl.pallas_call(functools.partial(kernel, N, T, K, F, start), out_shape=[j...]
    psum x1 -> x0, waiting for transfers between devices: 41.8 us -> none  [per_device(): features = lax.psum(part, 'tensor')]
  transfers between devices with their start and end apart: 1 -> 0, of which waited for: 1 -> 0; matrix products, arithmetic and copies ran while one was open for 0% -> 0% of each run, Pallas kernels for 0% -> 0%
where the time goes in v2:
time: 221 us; the launch traced here: 220 us
  Pallas kernels  216 us (98%)
  matrix products  2.73 us (1%)
    pallas_call x1, Pallas kernels, gather_and_project(): pl.pallas_call(functools.partial(kernel, N, T, K, F, start), out_shape=[j...  216 us

profile of v2, /device:TPU:0, one launch (start us, length us, event | category | flops | bytes accessed | tf_op | source)
XLA Modules:
  0.0 220.3 jit_solution(14397579635585669223)
XLA Ops:
  0.0 216.4 %shard_map.91 = (f32[192,128]{1,0:T(8,128)}, bf16[64,8192]{1,0:T(8,128)(2,1)}) custom-call(bf16[192,4096]{1,0:T(8,128)(2,1)} %x_ref.1, bf16[192,4096]{1,0:T(8,128)(2,1)} %cot_ref.1, bf16[768,3584]{1,0:T(8,128)(2,1)} %gate_ref.1, bf16[768,3584]{1,0:T(8,128)(2,1)} %up_ref.1, bf16[14,256,512]{2,1,0:T(8,128)(2,1)} %bitcast.9, bf16[4096,128]{1,0:T(8,128)(2,1)} %pm_ref.1, ...), custom_call_target="tpu_custom_call" | custom-call | tf_op jit(solution)/shard_map/pallas_call | solution.py:408
  216.4 1.1 reshape.14
  217.5 0.1 reshape.15
  217.6 2.7 %fusion = f32[3,64]{1,0:T(4,128)} fusion(f32[3,8192]{1,0:T(4,128)S(1)} %reshape.15, bf16[64,8192]{1,0:T(8,128)(2,1)} %get-tuple-element.8), kind=kOutput, calls=%fused_computation.1 | convolution fusion | flops 18874368 | bytes 1147648 | tf_op jit(solution)/shard_map/dot_general | solution.py:468
  (1 shorter events, 0.0 us)

commit v3 on v2

--- a/solution.py
+++ b/solution.py
@@ -10,7 +10,7 @@
 
 MESH = pl.DeviceIdType.MESH
 WINDOW = 14
-AHEAD = 4
+AHEAD = 6
 EARLY = 5
 
 

time: 221 us -> 211 us (0.955)
  Pallas kernels: 216 us -> 207 us
    pallas_call x1, Pallas kernels: 216 us -> 207 us  [gather_and_project(): pl.pallas_call(functools.partial(kernel, N, T, K, F, start), out_shape=[j...]
where the time goes in v3:
time: 211 us
  Pallas kernels  207 us (98%)
  matrix products  2.73 us (1%)
    pallas_call x1, Pallas kernels, gather_and_project(): pl.pallas_call(functools.partial(kernel, N, T, K, F, start), out_shape=[j...  207 us

profile of v3, /device:TPU:0, one launch (start us, length us, event | category | flops | bytes accessed | tf_op | source)
XLA Modules:
  0.0 211.2 jit_solution(3491134308860181134)
XLA Ops:
  0.0 207.2 %shard_map.91 = (f32[192,128]{1,0:T(8,128)}, bf16[64,8192]{1,0:T(8,128)(2,1)}) custom-call(bf16[192,4096]{1,0:T(8,128)(2,1)} %x_ref.1, bf16[192,4096]{1,0:T(8,128)(2,1)} %cot_ref.1, bf16[768,3584]{1,0:T(8,128)(2,1)} %gate_ref.1, bf16[768,3584]{1,0:T(8,128)(2,1)} %up_ref.1, bf16[14,256,512]{2,1,0:T(8,128)(2,1)} %bitcast.9, bf16[4096,128]{1,0:T(8,128)(2,1)} %pm_ref.1, ...), custom_call_target="tpu_custom_call" | custom-call | tf_op jit(solution)/shard_map/pallas_call | solution.py:408
  207.2 1.1 reshape.14
  208.3 0.1 reshape.15
  208.4 2.7 %fusion = f32[3,64]{1,0:T(4,128)} fusion(f32[3,8192]{1,0:T(4,128)S(1)} %reshape.15, bf16[64,8192]{1,0:T(8,128)(2,1)} %get-tuple-element.8), kind=kOutput, calls=%fused_computation.1 | convolution fusion | flops 18874368 | bytes 1147648 | tf_op jit(solution)/shard_map/dot_general | solution.py:468
  (1 shorter events, 0.0 us)
